TPU v7x, 128 devices: a whole 4x4x4 slice. The times are simulated.
128 devices in a mesh: grp: 4 (over y_lo, core), col: 32 (over x, y_hi, z).
Axes of the slice: x: 4, y: 4 (y_hi: 2, y_lo: 2; y = y_hi * 2 + y_lo), z: 4, core: 2. Of those that a mesh axis runs over, the one named last changes fastest.
Arguments:
- amplitudes: bfloat16 [768, 262144], P(('grp', 'col')), may hold values from -6 to 6
- integrals: bfloat16 [4096, 262144], P('grp', 'col'), may hold values from -0.01171875 to 0.01171875
Outputs:
- ladder: float32 [768, 4096], P('col', 'grp')
All inputs are finite; a program needn't handle non-finite values.
Results may differ from a plain program's by a relative error of at most 0.0003.
Values may be sent and summed in bfloat16 or wider, within the bound.
A program may use at most 128 MiB of HBM per device.

v0:
```python
import jax
import jax.numpy as jnp
from jax import lax
from jax.sharding import PartitionSpec as P


def per_device(amplitudes, integrals):
    groups = lax.axis_size("grp")
    columns = lax.axis_size("col")
    stacked = lax.all_gather(amplitudes, "grp", axis=0, tiled=True)
    received = lax.all_to_all(stacked, "col", split_axis=1, concat_axis=0, tiled=True)
    local_rows = amplitudes.shape[0]
    reordered = received.reshape(columns, groups, local_rows, received.shape[1])
    panel_rows = jnp.transpose(reordered, (1, 0, 2, 3)).reshape(
        columns * groups * local_rows, received.shape[1]
    )
    products = lax.psum_scatter(
        lax.dot_general(
            panel_rows, integrals, (((1,), (1,)), ((), ())), preferred_element_type=jnp.float32
        ),
        "col",
        scatter_dimension=0,
        tiled=True,
    )
    return 0.5 * products


def solution(mesh):
    return jax.shard_map(
        per_device,
        mesh=mesh,
        in_specs=(P(("grp", "col"), None), P("grp", "col")),
        out_specs=P("col", "grp"),
        check_vma=False,
    )
```

profile of v0, /device:TPU:18, one launch (start us, length us, event | category | flops | bytes accessed | tf_op | source)
XLA Modules:
  0.0 682.5 jit_solution(2358948042734618038)
XLA Ops:
  6.5 0.0 all-gather.3.cloned.1.call-start
  6.5 0.7 all-gather.3.cloned.1.call-update
  7.3 0.0 reduce-scatter.2.cloned.1.call-start
  7.3 153.3 %all-gather.3.cloned.1.call-done = bf16[4,6,262144]{2,1,0:T(8,128)(2,1)} async-done(((bf16[1,6,262144]{2,1,0:T(8,128)(2,1)}), bf16[4,6,262144]{2,1,0:T(8,128)(2,1)}) %all-gather.3.cloned.1.call-update) | async-done | bytes 12582928 | tf_op jit(solution)/shard_map/all_gather | solution.py:10
  160.6 22.6 %all_to_all.12 = bf16[24,32,8192]{2,1,0:T(8,128)(2,1)} reshape(bf16[4,6,262144]{2,1,0:T(8,128)(2,1)} %all-gather.3.cloned.1.call-done) | data formatting | bytes 25165824 | tf_op jit(solution)/shard_map/all_to_all | solution.py:11
  183.2 11.5 %copy.6 = bf16[24,32,8192]{2,0,1:T(8,128)(2,1)S(1)} copy(bf16[24,32,8192]{2,1,0:T(8,128)(2,1)} %all_to_all.12) | data formatting | bytes 25165824 | tf_op jit(solution)/shard_map/all_to_all | solution.py:11
  194.7 151.3 %all_to_all.16 = bf16[24,32,8192]{2,0,1:T(8,128)(2,1)S(1)} all-to-all(bf16[24,32,8192]{2,0,1:T(8,128)(2,1)S(1)} %copy.6), channel_id=1, replica_groups=mesh['grp'=4,'col'=32] {'col'}, dimensions={1} | all-to-all | bytes 25165824 | tf_op jit(solution)/shard_map/all_to_all | solution.py:11
  346.0 15.9 %copy.7 = bf16[24,32,8192]{2,1,0:T(8,128)(2,1)S(1)} copy(bf16[24,32,8192]{2,0,1:T(8,128)(2,1)S(1)} %all_to_all.16) | data formatting | bytes 25165824 | tf_op jit(solution)/shard_map/all_to_all | solution.py:11
  361.9 25.9 %copy.8 = bf16[4,32,6,8192]{3,2,1,0:T(8,128)(2,1)} copy(bf16[4,32,6,8192]{3,1,2,0:T(8,128)(2,1)S(1)} %bitcast.8) | data formatting | bytes 25165824 | tf_op jit(solution)/shard_map/transpose | solution.py:14
  387.8 17.5 %reshape.11 = bf16[768,8192]{1,0:T(8,128)(2,1)} reshape(bf16[4,32,6,8192]{3,2,1,0:T(8,128)(2,1)} %copy.8) | data formatting | bytes 25165824 | tf_op jit(solution)/shard_map/reshape | solution.py:14
  405.3 20.2 %fusion = f32[768,1024]{1,0:T(8,128)} fusion(bf16[768,8192]{1,0:T(8,128)(2,1)} %reshape.11, bf16[1024,8192]{1,0:T(8,128)(2,1)} %param.3), kind=kOutput, calls=%fused_computation.1 | convolution fusion | flops 12884901888 | bytes 32505856 | tf_op jit(solution)/shard_map/dot_general | solution.py:18
  425.6 0.0 reduce-scatter.2.cloned.1.call-update
  425.6 248.5 %reduce-scatter.2.cloned.1.call-done = f32[24,1024]{1,0:T(8,128)} async-done(((f32[768,1024]{1,0:T(8,128)}), f32[24,1024]{1,0:T(8,128)}) %reduce-scatter.2.cloned.1.call-update) | async-done | bytes 98320 | tf_op jit(solution)/shard_map/reduce_scatter | solution.py:17
  674.1 1.5 broadcast_multiply_fusion
Async XLA Ops:
  6.5 154.1 %all-gather.3.cloned.1.call-start = ((), (), s32[]{:S(2)}) async-start(), calls=%async_computation.3 | async-start | bytes 20971520 | tf_op jit(solution)/shard_map/all_gather | solution.py:10
  7.3 666.8 %reduce-scatter.2.cloned.1.call-start = ((), (), s32[]{:S(2)}) async-start(), calls=%async_computation.2 | async-start | bytes 3244032 | tf_op jit(solution)/shard_map/reduce_scatter | solution.py:17
Sparse Core Ops, SparseCore 0:
  9.0 151.5 all-gather.2
  425.7 248.3 reduce-scatter.1
where the time goes:
time: 686 us; the launch traced here: 682 us
  waiting for transfers between devices  403 us (59%)
  blocking collectives  151 us (22%)
  local copies, waits for them, and re-layouts  93.3 us (14%)
  matrix products  20.2 us (3%)
  between operations  13.4 us (2%)
    reduce_scatter x1, waiting for transfers between devices, per_device(): lax.psum_scatter(lax.dot_general(panel_rows, integrals, (((1,), (1,)), ((...  249 us
    all_gather x1, waiting for transfers between devices, per_device(): stacked = lax.all_gather(amplitudes, 'grp', axis=0, tiled=True)  153 us
    all_to_all x1, blocking collectives, per_device(): lax.all_to_all(stacked, 'col', split_axis=1, concat_axis=0, tiled=True)  151 us
    all_to_all x3, local copies, waits for them, and re-layouts, per_device(): lax.all_to_all(stacked, 'col', split_axis=1, concat_axis=0, tiled=True)  49.9 us
    transpose x1, local copies, waits for them, and re-layouts, per_device(): jnp.transpose(reordered, (1, 0, 2, 3))  25.9 us
    dot_general x1, matrix products, per_device(): lax.dot_general(panel_rows, integrals, (((1,), (1,)), ((), ())), preferre...  20.2 us
    reshape x1, local copies, waits for them, and re-layouts, per_device(): jnp.transpose(reordered, (1, 0, 2, 3))  17.5 us
  transfers between devices with their start and end apart: 2, of which 2 were waited for; matrix products, arithmetic and copies ran while one was open for 0% of the time, Pallas kernels for 0%

commit v1 on v0

v1 whole, which is shorter than its diff:
```python
import jax
import jax.numpy as jnp
from jax import lax
from jax.experimental import pallas as pl
from jax.experimental.pallas import tpu as pltpu
from jax.sharding import PartitionSpec as P

MESH = pl.DeviceIdType.MESH
ROWS = 6
BLOCK = 8 * ROWS
STEP = 4 * BLOCK
STEPS = 4
PIECE = 24
KPARTS = 4
LEVEL = 99


def device(x, y, z, s):
    return ((y % 2) * 2 + s, (x * 2 + y // 2) * 4 + z)


def across(y):
    return (y + 3 + 2 * (y % 2)) % 4


def kernel(amp, integrals_hbm, out, integrals, landed, wide, panel, parts, from_z, reduced, from_xy,
           load_sem, send_sem, land_sem, pair_send, sib_send, block_sem, z_send, z_recv, xy_send, xy_recv):
    g = lax.axis_index("grp")
    c = lax.axis_index("col")
    x, y, z, s = c // 8, (c // 4) % 2 * 2 + g // 2, c % 4, g % 2
    y_hi, y_lo = y // 2, y % 2
    kind = (y_lo + y_hi) % 2
    cols = integrals.shape[1]
    part = cols // KPARTS
    core = x % 2
    own = jnp.where(s == core, 1, 0)
    pair = device(x, y + 1 - 2 * y_lo, z, s)
    sibling = device(x, y, z, 1 - s)

    load = pltpu.make_async_copy(integrals_hbm, integrals, load_sem)
    load.start()

    bar = pltpu.get_barrier_semaphore()

    def greet(i, _):
        src_x = 2 * (i % 2) + s
        src_y = jnp.where((i // 2) % 2 == 0, y, across(y))
        src_z = (i // 4) % 4
        src_s = i // 16
        other = jnp.logical_not((src_x == x) & (src_y == y) & (src_z == z) & (src_s == s))

        @pl.when(other)
        def _():
            pl.semaphore_signal(bar, inc=1, device_id=device(src_x, src_y, src_z, src_s), device_id_type=MESH)

        return 0

    lax.fori_loop(0, 32, greet, 0)
    pl.semaphore_signal(bar, inc=1, device_id=pair, device_id_type=MESH)
    pl.semaphore_signal(bar, inc=1, device_id=sibling, device_id_type=MESH)
    for d in range(1, 4):
        pl.semaphore_signal(bar, inc=1, device_id=device(x, y, (z + d) % 4, s), device_id_type=MESH)
    for d in range(1, 8):
        pl.semaphore_signal(bar, inc=1, device_id=device((x + d % 4) % 4, (y + 2 * (d // 4)) % 4, z, s), device_id_type=MESH)
    pl.semaphore_wait(bar, 44 - own)

    my_step = s * 2 + x // 2

    def send_all():
        def one(n, _):
            k, i = n // 32, n % 32
            j, m = i // 2, i % 2
            dx = j % 4
            dz = (j // 4 + j) % 4
            to_x = jnp.where(m == 0, x + dx, x - dx + 4) % 4
            to_z = jnp.where(m == 0, z + dz, z - dz + 4) % 4
            to_y = jnp.where(m == 0, y, across(y))
            to_col = (to_x * 2 + to_y // 2) * 4 + to_z
            src = amp.at[:, pl.ds(pl.multiple_of(to_col * cols + k * part, 128), part)]
            slot = (my_step * KPARTS + k) * 8 + y_hi * 4 + z
            here = jnp.logical_and(i == 0, own == 1)

            @pl.when(here)
            def _():
                pltpu.make_async_copy(src, landed.at[slot], land_sem.at[my_step, k]).start()

            @pl.when(jnp.logical_not(here))
            def _():
                pltpu.make_async_remote_copy(
                    src_ref=src, dst_ref=landed.at[slot], send_sem=send_sem, recv_sem=land_sem.at[my_step, k],
                    device_id=device(to_x, to_y, to_z, core), device_id_type=MESH,
                ).start()

            return 0

        lax.fori_loop(0, 32 * KPARTS, one, 0)

    def block_ref(t, kk, ss, k):
        return panel.at[k, pl.ds(pl.multiple_of(t * STEP + kk * 2 * BLOCK + ss * BLOCK, 16), BLOCK), :]

    def forward(t, kk, k, to, sem):
        ref = block_ref(t, kk, s, k)
        return pltpu.make_async_remote_copy(
            src_ref=ref, dst_ref=ref, send_sem=sem, recv_sem=block_sem.at[t, kk * 2 + s, k],
            device_id=to, device_id_type=MESH,
        )

    def wait_block(t, kk, ss, k):
        ref = block_ref(t, kk, ss, k)
        pltpu.make_async_copy(ref, ref, block_sem.at[t, kk * 2 + ss, k]).wait()

    def take(t, k):
        base = (t * KPARTS + k) * 8
        eight = landed.at[pl.ds(base, 8)]
        pltpu.make_async_copy(eight, eight, land_sem.at[t, k]).wait()
        row0 = pl.multiple_of(t * STEP + kind * 2 * BLOCK + s * BLOCK, 16)
        width = min(part, 512)

        def repack(i, _):
            lanes = pl.ds(pl.multiple_of(i * width, width), width)
            for m in range(8):
                wide[pl.ds(m * ROWS, ROWS), :] = landed[base + m, :, lanes].astype(jnp.float32)
            panel[k, pl.ds(row0, BLOCK), lanes] = wide[...].astype(jnp.bfloat16)
            return 0

        lax.fori_loop(0, part // width, repack, 0)
        forward(t, kind, k, pair, pair_send.at[t, k]).start()
        forward(t, kind, k, sibling, sib_send.at[t, 0, k]).start()

    def relay(t, k):
        wait_block(t, 1 - kind, s, k)
        forward(t, 1 - kind, k, sibling, sib_send.at[t, 1, k]).start()

    def gather_sibling(t):
        def one(k, _):
            wait_block(t, kind, 1 - s, k)
            wait_block(t, 1 - kind, 1 - s, k)
            return 0

        lax.fori_loop(0, KPARTS, one, 0)

    def multiply(t):
        def tile(n, _):
            lanes = pl.ds(pl.multiple_of(n * 256, 256), 256)

            def add(k, total):
                return total + lax.dot_general(
                    panel[k, pl.ds(t * STEP, STEP), :],
                    integrals[lanes, pl.ds(pl.multiple_of(k * part, part), part)],
                    (((1,), (1,)), ((), ())),
                    preferred_element_type=jnp.float32,
                )

            total = lax.fori_loop(0, KPARTS, add, jnp.zeros((STEP, 256), jnp.float32))
            for kk in range(2):
                for r in range(2):
                    for u in range(2):
                        row = (kk * 2 + r) * BLOCK + u * PIECE
                        parts[t, 2 * r + u, pl.ds(kk * PIECE, PIECE), lanes] = total[row:row + PIECE]
            return 0

        lax.fori_loop(0, integrals.shape[0] // 256, tile, 0)

    def z_copy(t, d):
        return pltpu.make_async_remote_copy(
            src_ref=parts.at[t, (z + d) % 4], dst_ref=from_z.at[t, d - 1],
            send_sem=z_send.at[t, d - 1], recv_sem=z_recv.at[t, d - 1],
            device_id=device(x, y, (z + d) % 4, s), device_id_type=MESH,
        )

    def send_z(t):
        for d in (1, 3, 2):
            z_copy(t, d).start()

    u = z % 2

    def owner(t, kk):
        return 2 * ((kk + u) % 2) + t // 2, t % 2

    def xy_copy(t, kk):
        to_x, to_yhi = owner(t, kk)
        d = (x - to_x + 4) % 4 + 4 * ((y_hi + to_yhi) % 2)
        return d, pltpu.make_async_remote_copy(
            src_ref=reduced.at[t, pl.ds(kk * PIECE, PIECE)], dst_ref=from_xy.at[d],
            send_sem=xy_send.at[t, kk], recv_sem=xy_recv.at[d],
            device_id=device(to_x, to_yhi * 2 + y_lo, z, s), device_id_type=MESH,
        )

    def reduce_z(t):
        for d in range(1, 4):
            z_copy(t, d).wait_recv()
        reduced[t] = 0.5 * (parts[t, z] + from_z[t, 0] + from_z[t, 1] + from_z[t, 2])
        for kk in range(2):
            d, cp = xy_copy(t, kk)

            @pl.when(d != 0)
            def _():
                cp.start()

            @pl.when(d == 0)
            def _():
                from_xy[0] = reduced[t, pl.ds(kk * PIECE, PIECE)]

    @pl.when(s == 0)
    def _():
        send_all()

    for k in range(KPARTS):
        for t in (0, 1):
            take(t, k)

    @pl.when(s == 1)
    def _():
        send_all()

    for k in range(KPARTS):
        for t in (0, 1):
            relay(t, k)
    for t in (2, 3):
        for k in range(KPARTS):
            take(t, k)
    load.wait()
    for t in (0, 1):
        gather_sibling(t)
        multiply(t)
        send_z(t)
    for k in range(KPARTS):
        relay(2, k)
    reduce_z(0)
    gather_sibling(2)
    multiply(2)
    send_z(2)
    reduce_z(1)
    for k in range(KPARTS):
        relay(3, k)
    gather_sibling(3)
    multiply(3)
    send_z(3)
    reduce_z(2)
    reduce_z(3)

    total = from_xy[0]
    for d in range(1, 8):
        pltpu.make_async_copy(from_xy.at[d], from_xy.at[d], xy_recv.at[d]).wait()
        total = total + from_xy[d]
    out[...] = total

    many = 32 * KPARTS

    @pl.when(own == 1)
    def _():
        left = landed.at[pl.ds(0, many - KPARTS)]
        pltpu.make_async_copy(left, left, send_sem).wait()

    @pl.when(own == 0)
    def _():
        left = landed.at[pl.ds(0, many)]
        pltpu.make_async_copy(left, left, send_sem).wait()

    for t in range(STEPS):
        for k in range(KPARTS):
            forward(t, kind, k, pair, pair_send.at[t, k]).wait_send()
            forward(t, kind, k, sibling, sib_send.at[t, 0, k]).wait_send()
            forward(t, 1 - kind, k, sibling, sib_send.at[t, 1, k]).wait_send()
        for d in range(1, 4):
            z_copy(t, d).wait_send()
        for kk in range(2):
            d, cp = xy_copy(t, kk)

            @pl.when(d != 0)
            def _():
                cp.wait_send()


def per_device(amplitudes, integrals):
    ab, cols = integrals.shape
    part = cols // KPARTS
    return pl.pallas_call(
        kernel,
        out_shape=jax.ShapeDtypeStruct((PIECE, ab), jnp.float32),
        in_specs=[pl.BlockSpec(memory_space=pl.ANY)] * 2,
        out_specs=pl.BlockSpec(memory_space=pltpu.VMEM),
        scratch_shapes=[
            pltpu.VMEM((ab, cols), jnp.bfloat16),
            pltpu.VMEM((32 * KPARTS, ROWS, part), jnp.bfloat16),
            pltpu.VMEM((BLOCK, min(part, 512)), jnp.float32),
            pltpu.VMEM((KPARTS, STEPS * STEP, part), jnp.bfloat16),
            pltpu.VMEM((STEPS, 4, 2 * PIECE, ab), jnp.float32),
            pltpu.VMEM((STEPS, 3, 2 * PIECE, ab), jnp.float32),
            pltpu.VMEM((STEPS, 2 * PIECE, ab), jnp.float32),
            pltpu.VMEM((8, PIECE, ab), jnp.float32),
            pltpu.SemaphoreType.DMA,
            pltpu.SemaphoreType.DMA,
            pltpu.SemaphoreType.DMA((STEPS, KPARTS)),
            pltpu.SemaphoreType.DMA((STEPS, KPARTS)),
            pltpu.SemaphoreType.DMA((STEPS, 2, KPARTS)),
            pltpu.SemaphoreType.DMA((STEPS, 4, KPARTS)),
            pltpu.SemaphoreType.DMA((STEPS, 3)),
            pltpu.SemaphoreType.DMA((STEPS, 3)),
            pltpu.SemaphoreType.DMA((STEPS, 2)),
            pltpu.SemaphoreType.DMA((8,)),
        ],
        compiler_params=pltpu.CompilerParams(
            collective_id=0, has_side_effects=True, vmem_limit_bytes=60 * 2**20
        ),
        cost_estimate=pl.CostEstimate(
            flops=2 * STEPS * STEP * ab * cols, bytes_accessed=2 * ab * cols, transcendentals=0
        ),
        name="ladder",
    )(amplitudes, integrals)


def solution(mesh):
    return jax.shard_map(
        per_device,
        mesh=mesh,
        in_specs=(P(("grp", "col"), None), P("grp", "col")),
        out_specs=P("col", "grp"),
        check_vma=False,
    )
```

time: 686 us -> 125 us (0.18)
  waiting for transfers between devices: 403 us -> 0 us
  blocking collectives: 151 us -> 0 us
  Pallas kernels: 0 us -> 123 us
  local copies, waits for them, and re-layouts: 93.3 us -> 1.54 us
  matrix products: 20.2 us -> 0 us
  between operations: 13.4 us -> 0.01 us
    reduce_scatter x1 -> x0, waiting for transfers between devices: 249 us -> none  [per_device(): lax.psum_scatter(lax.dot_general(panel_rows, integrals, (((1,), (1,)), ((...]
    all_gather x1 -> x0, waiting for transfers between devices: 153 us -> none  [per_device(): stacked = lax.all_gather(amplitudes, 'grp', axis=0, tiled=True)]
    all_to_all x1 -> x0, blocking collectives: 151 us -> none  [per_device(): lax.all_to_all(stacked, 'col', split_axis=1, concat_axis=0, tiled=True)]
    pallas_call x0 -> x1, Pallas kernels: none -> 123 us  [per_device(): pl.pallas_call(kernel, out_shape=jax.ShapeDtypeStruct((PIECE, ab), jnp.fl...]
    all_to_all x3 -> x0, local copies, waits for them, and re-layouts: 49.9 us -> none  [per_device(): lax.all_to_all(stacked, 'col', split_axis=1, concat_axis=0, tiled=True)]
    transpose x1 -> x0, local copies, waits for them, and re-layouts: 25.9 us -> none  [per_device(): jnp.transpose(reordered, (1, 0, 2, 3))]
    dot_general x1 -> x0, matrix products: 20.2 us -> none  [per_device(): lax.dot_general(panel_rows, integrals, (((1,), (1,)), ((), ())), preferre...]
    reshape x1 -> x0, local copies, waits for them, and re-layouts: 17.5 us -> none  [per_device(): jnp.transpose(reordered, (1, 0, 2, 3))]
  transfers between devices with their start and end apart: 2 -> 0, of which waited for: 2 -> 0; matrix products, arithmetic and copies ran while one was open for 0% -> 0% of each run, Pallas kernels for 0% -> 0%
where the time goes in v1:
time: 125 us
  Pallas kernels  123 us (98%)
  local copies, waits for them, and re-layouts  1.54 us (1%)
    pallas_call x1, Pallas kernels, per_device(): pl.pallas_call(kernel, out_shape=jax.ShapeDtypeStruct((PIECE, ab), jnp.fl...  123 us

profile of v1, /device:TPU:18, one launch (start us, length us, event | category | flops | bytes accessed | tf_op | source)
XLA Modules:
  0.0 124.7 jit_solution(373124706318266270)
XLA Ops:
  0.0 123.1 %ladder.1 = f32[24,1024]{1,0:T(8,128)} custom-call(bf16[6,262144]{1,0:T(8,128)(2,1)} %amp.1, bf16[1024,8192]{1,0:T(8,128)(2,1)} %integrals_hbm.1), custom_call_target="tpu_custom_call" | custom-call | flops 12884901888 | bytes 16777216 | tf_op jit(solution)/shard_map/ladder/pallas_call | solution.py:278
  123.1 1.5 %copy.4 = f32[24,1024]{1,0:T(8,128)} copy(f32[24,1024]{1,0:T(8,128)} %ladder.1) | data formatting | bytes 196608

commit v2 on v1

v2 whole, which is shorter than its diff:
```python
import jax
import jax.numpy as jnp
from jax import lax
from jax.experimental import pallas as pl
from jax.experimental.pallas import tpu as pltpu
from jax.sharding import PartitionSpec as P

MESH = pl.DeviceIdType.MESH
ROWS = 6
BLOCK = 8 * ROWS
STEP = 4 * BLOCK
STEPS = 4
PIECE = 24
KPARTS = 8
MPARTS = 4
WIDE = 512
AHEAD = 3


def device(x, y, z, s):
    return ((y % 2) * 2 + s, (x * 2 + y // 2) * 4 + z)


def across(y):
    return (y + 3 + 2 * (y % 2)) % 4


def kernel(amp, integrals_hbm, out, integrals, landed, wide, panel, parts, from_z, reduced, from_x, summed, from_y,
           load_sem, send_sem, land_sem, pair_send, sib_send, block_sem, z_send, z_recv, x_send, x_recv, y_send, y_recv):
    g = lax.axis_index("grp")
    c = lax.axis_index("col")
    x, y, z, s = c // 8, (c // 4) % 2 * 2 + g // 2, c % 4, g % 2
    y_hi, y_lo = y // 2, y % 2
    kind = (y_lo + y_hi) % 2
    cols = integrals.shape[1]
    part = cols // KPARTS
    per = KPARTS // MPARTS
    tiles = integrals.shape[0] // WIDE
    core = x % 2
    own = jnp.where(s == core, 1, 0)
    pair = device(x, y + 1 - 2 * y_lo, z, s)
    sibling = device(x, y, z, 1 - s)

    load = pltpu.make_async_copy(integrals_hbm, integrals, load_sem)
    load.start()

    bar = pltpu.get_barrier_semaphore()

    def greet(i, _):
        src_x = 2 * (i % 2) + s
        src_y = jnp.where((i // 2) % 2 == 0, y, across(y))
        src_z = (i // 4) % 4
        src_s = i // 16
        other = jnp.logical_not((src_x == x) & (src_y == y) & (src_z == z) & (src_s == s))

        @pl.when(other)
        def _():
            pl.semaphore_signal(bar, inc=1, device_id=device(src_x, src_y, src_z, src_s), device_id_type=MESH)

        return 0

    lax.fori_loop(0, 32, greet, 0)
    pl.semaphore_signal(bar, inc=1, device_id=pair, device_id_type=MESH)
    pl.semaphore_signal(bar, inc=1, device_id=sibling, device_id_type=MESH)
    for d in range(1, 4):
        pl.semaphore_signal(bar, inc=1, device_id=device(x, y, (z + d) % 4, s), device_id_type=MESH)
        pl.semaphore_signal(bar, inc=1, device_id=device((x + d) % 4, y, z, s), device_id_type=MESH)
    pl.semaphore_signal(bar, inc=1, device_id=device(x, (y + 2) % 4, z, s), device_id_type=MESH)
    parts[...] = jnp.zeros_like(parts)
    pl.semaphore_wait(bar, 41 - own)

    my_step = s * 2 + x // 2

    def send_part(k):
        def one(i, _):
            j, m = i // 2, i % 2
            dx = j % 4
            dz = (j // 4 + j) % 4
            to_x = jnp.where(m == 0, x + dx, x - dx + 4) % 4
            to_z = jnp.where(m == 0, z + dz, z - dz + 4) % 4
            to_y = jnp.where(m == 0, y, across(y))
            to_col = (to_x * 2 + to_y // 2) * 4 + to_z
            src = amp.at[:, pl.ds(pl.multiple_of(to_col * cols + k * part, 128), part)]
            slot = (my_step * KPARTS + k) * 8 + y_hi * 4 + z
            here = jnp.logical_and(i == 0, own == 1)

            @pl.when(here)
            def _():
                pltpu.make_async_copy(src, landed.at[slot], land_sem.at[my_step, k]).start()

            @pl.when(jnp.logical_not(here))
            def _():
                pltpu.make_async_remote_copy(
                    src_ref=src, dst_ref=landed.at[slot], send_sem=send_sem, recv_sem=land_sem.at[my_step, k],
                    device_id=device(to_x, to_y, to_z, core), device_id_type=MESH,
                ).start()

            return 0

        lax.fori_loop(0, 32, one, 0)

    def send_parts(who, first, last):
        if first < last:
            @pl.when(s == who)
            def _():
                lax.fori_loop(first, last, lambda k, _: (send_part(k), 0)[1], 0)

    def block_ref(t, kk, ss, k):
        rows = pl.ds(pl.multiple_of(t * STEP + kk * 2 * BLOCK + ss * BLOCK, 16), BLOCK)
        return panel.at[k // per, rows, pl.ds(pl.multiple_of(k % per * part, 128), part)]

    def forward(t, kk, k, to, sem):
        ref = block_ref(t, kk, s, k)
        return pltpu.make_async_remote_copy(
            src_ref=ref, dst_ref=ref, send_sem=sem, recv_sem=block_sem.at[t, kk * 2 + s, k],
            device_id=to, device_id_type=MESH,
        )

    def wait_block(t, kk, ss, k):
        ref = block_ref(t, kk, ss, k)
        pltpu.make_async_copy(ref, ref, block_sem.at[t, kk * 2 + ss, k]).wait()

    def take(t, k):
        base = (t * KPARTS + k) * 8
        eight = landed.at[pl.ds(base, 8)]
        pltpu.make_async_copy(eight, eight, land_sem.at[t, k]).wait()
        row0 = pl.multiple_of(t * STEP + kind * 2 * BLOCK + s * BLOCK, 16)
        width = min(part, 512)

        def repack(i, _):
            lanes = pl.ds(pl.multiple_of(i * width, width), width)
            to = pl.ds(pl.multiple_of(k % per * part + i * width, width), width)
            for m in range(8):
                wide[pl.ds(m * ROWS, ROWS), :] = landed[base + m, :, lanes].astype(jnp.float32)
            panel[k // per, pl.ds(row0, BLOCK), to] = wide[...].astype(jnp.bfloat16)
            return 0

        lax.fori_loop(0, part // width, repack, 0)
        forward(t, kind, k, pair, pair_send.at[t, k]).start()
        forward(t, kind, k, sibling, sib_send.at[t, 0, k]).start()

    def relay(t, k):
        wait_block(t, 1 - kind, s, k)
        forward(t, 1 - kind, k, sibling, sib_send.at[t, 1, k]).start()

    def wait_sibling(t, k):
        wait_block(t, kind, 1 - s, k)
        wait_block(t, 1 - kind, 1 - s, k)

    def z_copy(t, n, d):
        return pltpu.make_async_remote_copy(
            src_ref=parts.at[t, (z + d) % 4, n], dst_ref=from_z.at[t, d - 1, n],
            send_sem=z_send.at[t, d - 1, n], recv_sem=z_recv.at[t, d - 1, n],
            device_id=device(x, y, (z + d) % 4, s), device_id_type=MESH,
        )

    def multiply(t, km):
        width = per * part

        def tile(n, _):
            lanes = pl.ds(pl.multiple_of(n * WIDE, WIDE), WIDE)
            total = lax.dot_general(
                panel[km, pl.ds(pl.multiple_of(t * STEP, 16), STEP), :],
                integrals[lanes, pl.ds(pl.multiple_of(km * width, width), width)],
                (((1,), (1,)), ((), ())),
                preferred_element_type=jnp.float32,
            )
            for kk in range(2):
                for r in range(2):
                    for u in range(2):
                        row = (kk * 2 + r) * BLOCK + u * PIECE
                        parts[t, 2 * r + u, n, pl.ds(kk * PIECE, PIECE), :] += total[row:row + PIECE]

            @pl.when(km == MPARTS - 1)
            def _():
                for d in (2, 1, 3):
                    z_copy(t, n, d).start()

            return 0

        lax.fori_loop(0, tiles, tile, 0)

    def multiply_steps(first, last, km):
        lax.fori_loop(first, last, lambda t, _: (multiply(t, km), 0)[1], 0)

    u = z % 2

    def x_copy(t, n, kk):
        to_x = 2 * ((kk + u) % 2) + t // 2
        d = (to_x - x + 4) % 4
        place = jnp.maximum(d, 1) - 1
        return d, pltpu.make_async_remote_copy(
            src_ref=reduced.at[t, n, pl.ds(kk * PIECE, PIECE)], dst_ref=from_x.at[t % 2, place, n],
            send_sem=x_send.at[t, n, kk], recv_sem=x_recv.at[t % 2, place, n],
            device_id=device(to_x, y, z, s), device_id_type=MESH,
        )

    def y_copy(n):
        return pltpu.make_async_remote_copy(
            src_ref=summed.at[1, n], dst_ref=from_y.at[n], send_sem=y_send.at[n], recv_sem=y_recv.at[n],
            device_id=device(x, (y + 2) % 4, z, s), device_id_type=MESH,
        )

    def reduce_z(t):
        def one(n, _):
            for d in range(1, 4):
                z_copy(t, n, d).wait_recv()
            reduced[t, n] = 0.5 * (parts[t, z, n] + from_z[t, 0, n] + from_z[t, 1, n] + from_z[t, 2, n])
            for kk in range(2):
                d, cp = x_copy(t, n, kk)
                pl.when(d != 0)(cp.start)
            return 0

        lax.fori_loop(0, tiles, one, 0)

    def reduce_x(t):
        @pl.when(x % 2 == t // 2)
        def _():
            kk = (x // 2 + u) % 2
            mine = jnp.where(y_hi == t % 2, 0, 1)

            def one(n, _):
                for d in range(3):
                    ref = from_x.at[t % 2, d, n]
                    pltpu.make_async_copy(ref, ref, x_recv.at[t % 2, d, n]).wait()
                rows = pl.ds(pl.multiple_of(kk * PIECE, 8), PIECE)
                summed[mine, n] = reduced[t, n, rows, :] + from_x[t % 2, 0, n] + from_x[t % 2, 1, n] + from_x[t % 2, 2, n]
                pl.when(mine == 1)(y_copy(n).start)
                return 0

            lax.fori_loop(0, tiles, one, 0)

    send_parts(0, 0, AHEAD)
    for k in range(KPARTS):
        take(0, k)
        take(1, k)
        send_parts(0, k + AHEAD, min(k + AHEAD + 1, KPARTS))
        if k >= 3:
            send_parts(1, k - 3, k - 2)
        if k >= 2:
            relay(0, k - 2)
            relay(1, k - 2)
        if k == 0:
            load.wait()
        if k >= 4 and k % per == 0:
            km = (k - 4) // per
            for kt in range(km * per, km * per + per):
                wait_sibling(0, kt)
                wait_sibling(1, kt)
            multiply_steps(0, 2, km)
    send_parts(1, KPARTS - 3, KPARTS)
    for k in range(KPARTS):
        take(2, k)
        if k < 2:
            relay(0, KPARTS - 2 + k)
            relay(1, KPARTS - 2 + k)
        if k in (2, 4):
            km = MPARTS - 2 + (k - 2) // 2
            for kt in range(km * per, km * per + per):
                wait_sibling(0, kt)
                wait_sibling(1, kt)
            multiply_steps(0, 2, km)

    def third(km, _):
        def one(i, _):
            take(3, km * per + i)
            relay(2, km * per + i)
            return 0

        lax.fori_loop(0, per, one, 0)
        lax.fori_loop(0, per, lambda i, _: (wait_sibling(2, km * per + i), 0)[1], 0)
        multiply(2, km)

        @pl.when(km < 2)
        def _():
            reduce_z(km)

        return 0

    lax.fori_loop(0, MPARTS, third, 0)

    def fourth(km, _):
        lax.fori_loop(0, per, lambda i, _: (relay(3, km * per + i), 0)[1], 0)
        lax.fori_loop(0, per, lambda i, _: (wait_sibling(3, km * per + i), 0)[1], 0)
        multiply(3, km)

        @pl.when(km < 2)
        def _():
            reduce_x(km)

        @pl.when(km == 2)
        def _():
            reduce_z(2)

        return 0

    lax.fori_loop(0, MPARTS, fourth, 0)
    reduce_x(2)
    reduce_z(3)
    reduce_x(3)

    for n in range(tiles):
        y_copy(n).wait_recv()
        out[:, n * WIDE:n * WIDE + WIDE] = summed[0, n] + from_y[n]

    many = 32 * KPARTS

    @pl.when(own == 1)
    def _():
        left = landed.at[pl.ds(0, many - KPARTS)]
        pltpu.make_async_copy(left, left, send_sem).wait()

    @pl.when(own == 0)
    def _():
        left = landed.at[pl.ds(0, many)]
        pltpu.make_async_copy(left, left, send_sem).wait()

    for t in range(STEPS):
        for k in range(KPARTS):
            forward(t, kind, k, pair, pair_send.at[t, k]).wait_send()
            forward(t, kind, k, sibling, sib_send.at[t, 0, k]).wait_send()
            forward(t, 1 - kind, k, sibling, sib_send.at[t, 1, k]).wait_send()
        for n in range(tiles):
            for d in range(1, 4):
                z_copy(t, n, d).wait_send()
            for kk in range(2):
                d, cp = x_copy(t, n, kk)
                pl.when(d != 0)(cp.wait_send)
    for n in range(tiles):
        y_copy(n).wait_send()


def per_device(amplitudes, integrals):
    ab, cols = integrals.shape
    part = cols // KPARTS
    tiles = ab // WIDE
    return pl.pallas_call(
        kernel,
        out_shape=jax.ShapeDtypeStruct((PIECE, ab), jnp.float32),
        in_specs=[pl.BlockSpec(memory_space=pl.ANY)] * 2,
        out_specs=pl.BlockSpec(memory_space=pltpu.VMEM),
        scratch_shapes=[
            pltpu.VMEM((ab, cols), jnp.bfloat16),
            pltpu.VMEM((32 * KPARTS, ROWS, part), jnp.bfloat16),
            pltpu.VMEM((BLOCK, min(part, 512)), jnp.float32),
            pltpu.VMEM((MPARTS, STEPS * STEP, cols // MPARTS), jnp.bfloat16),
            pltpu.VMEM((STEPS, 4, tiles, 2 * PIECE, WIDE), jnp.float32),
            pltpu.VMEM((STEPS, 3, tiles, 2 * PIECE, WIDE), jnp.float32),
            pltpu.VMEM((STEPS, tiles, 2 * PIECE, WIDE), jnp.float32),
            pltpu.VMEM((2, 3, tiles, PIECE, WIDE), jnp.float32),
            pltpu.VMEM((2, tiles, PIECE, WIDE), jnp.float32),
            pltpu.VMEM((tiles, PIECE, WIDE), jnp.float32),
            pltpu.SemaphoreType.DMA,
            pltpu.SemaphoreType.DMA,
            pltpu.SemaphoreType.DMA((STEPS, KPARTS)),
            pltpu.SemaphoreType.DMA((STEPS, KPARTS)),
            pltpu.SemaphoreType.DMA((STEPS, 2, KPARTS)),
            pltpu.SemaphoreType.DMA((STEPS, 4, KPARTS)),
            pltpu.SemaphoreType.DMA((STEPS, 3, tiles)),
            pltpu.SemaphoreType.DMA((STEPS, 3, tiles)),
            pltpu.SemaphoreType.DMA((STEPS, tiles, 2)),
            pltpu.SemaphoreType.DMA((2, 3, tiles)),
            pltpu.SemaphoreType.DMA((tiles,)),
            pltpu.SemaphoreType.DMA((tiles,)),
        ],
        compiler_params=pltpu.CompilerParams(
            collective_id=0, has_side_effects=True, vmem_limit_bytes=60 * 2**20
        ),
        cost_estimate=pl.CostEstimate(
            flops=2 * STEPS * STEP * ab * cols, bytes_accessed=2 * ab * cols, transcendentals=0
        ),
        name="ladder",
    )(amplitudes, integrals)


def solution(mesh):
    return jax.shard_map(
        per_device,
        mesh=mesh,
        in_specs=(P(("grp", "col"), None), P("grp", "col")),
        out_specs=P("col", "grp"),
        check_vma=False,
    )
```

time: 125 us -> 117 us (0.936)
  Pallas kernels: 123 us -> 115 us
    pallas_call x1, Pallas kernels: 123 us -> 115 us  [per_device(): pl.pallas_call(kernel, out_shape=jax.ShapeDtypeStruct((PIECE, ab), jnp.fl...]
where the time goes in v2:
time: 117 us
  Pallas kernels  115 us (98%)
  local copies, waits for them, and re-layouts  1.54 us (1%)
    pallas_call x1, Pallas kernels, per_device(): pl.pallas_call(kernel, out_shape=jax.ShapeDtypeStruct((PIECE, ab), jnp.fl...  115 us

profile of v2, /device:TPU:18, one launch (start us, length us, event | category | flops | bytes accessed | tf_op | source)
XLA Modules:
  0.0 116.6 jit_solution(15443826603900791148)
XLA Ops:
  0.0 115.1 %ladder.1 = f32[24,1024]{1,0:T(8,128)} custom-call(bf16[6,262144]{1,0:T(8,128)(2,1)} %amp.1, bf16[1024,8192]{1,0:T(8,128)(2,1)} %integrals_hbm.1), custom_call_target="tpu_custom_call" | custom-call | flops 12884901888 | bytes 16777216 | tf_op jit(solution)/shard_map/ladder/pallas_call | solution.py:337
  115.1 1.5 %copy.4 = f32[24,1024]{1,0:T(8,128)} copy(f32[24,1024]{1,0:T(8,128)} %ladder.1) | data formatting | bytes 196608

commit v3 on v2

--- a/solution.py
+++ b/solution.py
@@ -13,7 +13,8 @@
 PIECE = 24
 KPARTS = 8
 MPARTS = 4
-WIDE = 512
+HALF = 512
+FINE = 128
 AHEAD = 3
 
 
@@ -25,8 +26,10 @@
     return (y + 3 + 2 * (y % 2)) % 4
 
 
-def kernel(amp, integrals_hbm, out, integrals, landed, wide, panel, parts, from_z, reduced, from_x, summed, from_y,
-           load_sem, send_sem, land_sem, pair_send, sib_send, block_sem, z_send, z_recv, x_send, x_recv, y_send, y_recv):
+def kernel(amp, integrals_hbm, out, integrals, landed, wide, panel, total, parts, from_z, reduced, from_x, summed, from_y,
+           parts_b, from_xb, reduced_b, from_zb, summed_b, from_xyb,
+           load_sem, send_sem, land_sem, pair_send, sib_send, block_sem, z_send, z_recv, x_send, x_recv, y_send, y_recv,
+           xb_send, xb_recv, zb_send, zb_recv, xyb_send, xyb_recv):
     g = lax.axis_index("grp")
     c = lax.axis_index("col")
     x, y, z, s = c // 8, (c // 4) % 2 * 2 + g // 2, c % 4, g % 2
@@ -35,7 +38,6 @@
     cols = integrals.shape[1]
     part = cols // KPARTS
     per = KPARTS // MPARTS
-    tiles = integrals.shape[0] // WIDE
     core = x % 2
     own = jnp.where(s == core, 1, 0)
     pair = device(x, y + 1 - 2 * y_lo, z, s)
@@ -66,8 +68,11 @@
         pl.semaphore_signal(bar, inc=1, device_id=device(x, y, (z + d) % 4, s), device_id_type=MESH)
         pl.semaphore_signal(bar, inc=1, device_id=device((x + d) % 4, y, z, s), device_id_type=MESH)
     pl.semaphore_signal(bar, inc=1, device_id=device(x, (y + 2) % 4, z, s), device_id_type=MESH)
+    for d in range(1, 4):
+        pl.semaphore_signal(bar, inc=1, device_id=device((x + d) % 4, (y + 2) % 4, z, s), device_id_type=MESH)
     parts[...] = jnp.zeros_like(parts)
-    pl.semaphore_wait(bar, 41 - own)
+    parts_b[...] = jnp.zeros_like(parts_b)
+    pl.semaphore_wait(bar, 44 - own)
 
     my_step = s * 2 + x // 2
 
@@ -147,88 +152,163 @@
         wait_block(t, kind, 1 - s, k)
         wait_block(t, 1 - kind, 1 - s, k)
 
-    def z_copy(t, n, d):
+    def z_copy(t, d):
         return pltpu.make_async_remote_copy(
-            src_ref=parts.at[t, (z + d) % 4, n], dst_ref=from_z.at[t, d - 1, n],
-            send_sem=z_send.at[t, d - 1, n], recv_sem=z_recv.at[t, d - 1, n],
+            src_ref=parts.at[t, (z + d) % 4], dst_ref=from_z.at[t, d - 1],
+            send_sem=z_send.at[t, d - 1], recv_sem=z_recv.at[t, d - 1],
             device_id=device(x, y, (z + d) % 4, s), device_id_type=MESH,
+        )
+
+    def xb_copy(t, d):
+        return pltpu.make_async_remote_copy(
+            src_ref=parts_b.at[t, (x + d) % 4], dst_ref=from_xb.at[t, d - 1],
+            send_sem=xb_send.at[t, d - 1], recv_sem=xb_recv.at[t, d - 1],
+            device_id=device((x + d) % 4, y, z, s), device_id_type=MESH,
         )
 
     def multiply(t, km):
         width = per * part
-
-        def tile(n, _):
-            lanes = pl.ds(pl.multiple_of(n * WIDE, WIDE), WIDE)
-            total = lax.dot_general(
+        last = km == MPARTS - 1
+
+        def half(n, _):
+            total[...] = lax.dot_general(
                 panel[km, pl.ds(pl.multiple_of(t * STEP, 16), STEP), :],
-                integrals[lanes, pl.ds(pl.multiple_of(km * width, width), width)],
+                integrals[pl.ds(pl.multiple_of(n * HALF, HALF), HALF), pl.ds(pl.multiple_of(km * width, width), width)],
                 (((1,), (1,)), ((), ())),
                 preferred_element_type=jnp.float32,
             )
-            for kk in range(2):
-                for r in range(2):
-                    for u in range(2):
-                        row = (kk * 2 + r) * BLOCK + u * PIECE
-                        parts[t, 2 * r + u, n, pl.ds(kk * PIECE, PIECE), :] += total[row:row + PIECE]
-
-            @pl.when(km == MPARTS - 1)
-            def _():
-                for d in (2, 1, 3):
-                    z_copy(t, n, d).start()
+
+            @pl.when(n == 0)
+            def _():
+                for kk in range(2):
+                    for r in range(2):
+                        for u in range(2):
+                            row = (kk * 2 + r) * BLOCK + u * PIECE
+                            parts[t, 2 * r + u, pl.ds(kk * PIECE, PIECE), :] += total[row:row + PIECE, :]
+
+                @pl.when(last)
+                def _():
+                    for d in (2, 1, 3):
+                        z_copy(t, d).start()
+
+            @pl.when(n == 1)
+            def _():
+                for q in range(4):
+                    for kk in range(2):
+                        for r in range(2):
+                            for u in range(2):
+                                row = (kk * 2 + r) * BLOCK + u * PIECE
+                                parts_b[t, q, 2 * r + u, pl.ds(kk * PIECE, PIECE), :] += total[
+                                    row:row + PIECE, q * FINE:q * FINE + FINE]
+
+                @pl.when(last)
+                def _():
+                    for d in (2, 1, 3):
+                        xb_copy(t, d).start()
 
             return 0
 
-        lax.fori_loop(0, tiles, tile, 0)
+        lax.fori_loop(0, 2, half, 0)
 
     def multiply_steps(first, last, km):
         lax.fori_loop(first, last, lambda t, _: (multiply(t, km), 0)[1], 0)
 
     u = z % 2
 
-    def x_copy(t, n, kk):
-        to_x = 2 * ((kk + u) % 2) + t // 2
-        d = (to_x - x + 4) % 4
+    def owner_x(t, kk):
+        return 2 * ((kk + u) % 2) + t // 2
+
+    def x_copy(t, kk):
+        d = (owner_x(t, kk) - x + 4) % 4
         place = jnp.maximum(d, 1) - 1
         return d, pltpu.make_async_remote_copy(
-            src_ref=reduced.at[t, n, pl.ds(kk * PIECE, PIECE)], dst_ref=from_x.at[t % 2, place, n],
-            send_sem=x_send.at[t, n, kk], recv_sem=x_recv.at[t % 2, place, n],
-            device_id=device(to_x, y, z, s), device_id_type=MESH,
-        )
-
-    def y_copy(n):
+            src_ref=reduced.at[t, pl.ds(kk * PIECE, PIECE)], dst_ref=from_x.at[t % 2, place],
+            send_sem=x_send.at[t, kk], recv_sem=x_recv.at[t % 2, place],
+            device_id=device(owner_x(t, kk), y, z, s), device_id_type=MESH,
+        )
+
+    def y_copy():
         return pltpu.make_async_remote_copy(
-            src_ref=summed.at[1, n], dst_ref=from_y.at[n], send_sem=y_send.at[n], recv_sem=y_recv.at[n],
+            src_ref=summed.at[1], dst_ref=from_y, send_sem=y_send, recv_sem=y_recv,
             device_id=device(x, (y + 2) % 4, z, s), device_id_type=MESH,
         )
 
     def reduce_z(t):
-        def one(n, _):
-            for d in range(1, 4):
-                z_copy(t, n, d).wait_recv()
-            reduced[t, n] = 0.5 * (parts[t, z, n] + from_z[t, 0, n] + from_z[t, 1, n] + from_z[t, 2, n])
-            for kk in range(2):
-                d, cp = x_copy(t, n, kk)
-                pl.when(d != 0)(cp.start)
-            return 0
-
-        lax.fori_loop(0, tiles, one, 0)
+        for d in range(1, 4):
+            z_copy(t, d).wait_recv()
+        reduced[t] = 0.5 * (parts[t, z] + from_z[t, 0] + from_z[t, 1] + from_z[t, 2])
+        for kk in range(2):
+            d, cp = x_copy(t, kk)
+            pl.when(d != 0)(cp.start)
 
     def reduce_x(t):
         @pl.when(x % 2 == t // 2)
         def _():
             kk = (x // 2 + u) % 2
             mine = jnp.where(y_hi == t % 2, 0, 1)
-
-            def one(n, _):
-                for d in range(3):
-                    ref = from_x.at[t % 2, d, n]
-                    pltpu.make_async_copy(ref, ref, x_recv.at[t % 2, d, n]).wait()
-                rows = pl.ds(pl.multiple_of(kk * PIECE, 8), PIECE)
-                summed[mine, n] = reduced[t, n, rows, :] + from_x[t % 2, 0, n] + from_x[t % 2, 1, n] + from_x[t % 2, 2, n]
-                pl.when(mine == 1)(y_copy(n).start)
-                return 0
-
-            lax.fori_loop(0, tiles, one, 0)
+            for d in range(3):
+                ref = from_x.at[t % 2, d]
+                pltpu.make_async_copy(ref, ref, x_recv.at[t % 2, d]).wait()
+            rows = pl.ds(pl.multiple_of(kk * PIECE, 8), PIECE)
+            summed[mine] = reduced[t, rows, :] + from_x[t % 2, 0] + from_x[t % 2, 1] + from_x[t % 2, 2]
+            pl.when(mine == 1)(y_copy().start)
+
+    def zb_copy(t, d):
+        return pltpu.make_async_remote_copy(
+            src_ref=reduced_b.at[t, (z + d) % 4], dst_ref=from_zb.at[t, d - 1],
+            send_sem=zb_send.at[t, d - 1], recv_sem=zb_recv.at[t, d - 1],
+            device_id=device(x, y, (z + d) % 4, s), device_id_type=MESH,
+        )
+
+    def reduce_xb(t):
+        for d in range(1, 4):
+            xb_copy(t, d).wait_recv()
+        reduced_b[t] = 0.5 * (parts_b[t, x] + from_xb[t, 0] + from_xb[t, 1] + from_xb[t, 2])
+        for d in (2, 1, 3):
+            zb_copy(t, d).start()
+
+    sender = x * 2 + y_hi
+
+    def xyb_copy(t, kk):
+        to_x = owner_x(t, kk)
+        here = (to_x == x) & (y_hi == t % 2)
+        return here, pltpu.make_async_remote_copy(
+            src_ref=summed_b.at[t, pl.ds(kk * PIECE, PIECE)], dst_ref=from_xyb.at[sender],
+            send_sem=xyb_send.at[t, kk], recv_sem=xyb_recv.at[sender],
+            device_id=device(to_x, (t % 2) * 2 + y_lo, z, s), device_id_type=MESH,
+        )
+
+    def reduce_zb(t):
+        for d in range(1, 4):
+            zb_copy(t, d).wait_recv()
+        summed_b[t] = reduced_b[t, z] + from_zb[t, 0] + from_zb[t, 1] + from_zb[t, 2]
+        for kk in range(2):
+            here, cp = xyb_copy(t, kk)
+            pl.when(jnp.logical_not(here))(cp.start)
+
+            @pl.when(here)
+            def _():
+                from_xyb[sender] = summed_b[t, pl.ds(kk * PIECE, PIECE), :]
+
+    def end_sends(t):
+        def one(k, _):
+            forward(t, kind, k, pair, pair_send.at[t, k]).wait_send()
+            forward(t, kind, k, sibling, sib_send.at[t, 0, k]).wait_send()
+            forward(t, 1 - kind, k, sibling, sib_send.at[t, 1, k]).wait_send()
+            return 0
+
+        lax.fori_loop(0, KPARTS, one, 0)
+
+    def end_sums(t):
+        for d in range(1, 4):
+            z_copy(t, d).wait_send()
+            xb_copy(t, d).wait_send()
+            zb_copy(t, d).wait_send()
+        for kk in range(2):
+            d, cp = x_copy(t, kk)
+            pl.when(d != 0)(cp.wait_send)
+            here, cp = xyb_copy(t, kk)
+            pl.when(jnp.logical_not(here))(cp.wait_send)
 
     send_parts(0, 0, AHEAD)
     for k in range(KPARTS):
@@ -274,6 +354,12 @@
         @pl.when(km < 2)
         def _():
             reduce_z(km)
+            reduce_xb(km)
+
+        @pl.when(km >= 2)
+        def _():
+            reduce_x(km - 2)
+            reduce_zb(km - 2)
 
         return 0
 
@@ -286,22 +372,38 @@
 
         @pl.when(km < 2)
         def _():
-            reduce_x(km)
+            end_sends(km)
+            end_sums(km)
+
+        @pl.when(km == 1)
+        def _():
+            reduce_z(2)
+            reduce_xb(2)
 
         @pl.when(km == 2)
         def _():
-            reduce_z(2)
+            reduce_x(2)
+            reduce_zb(2)
+            end_sends(2)
 
         return 0
 
     lax.fori_loop(0, MPARTS, fourth, 0)
-    reduce_x(2)
     reduce_z(3)
+    reduce_xb(3)
     reduce_x(3)
-
-    for n in range(tiles):
-        y_copy(n).wait_recv()
-        out[:, n * WIDE:n * WIDE + WIDE] = summed[0, n] + from_y[n]
+    reduce_zb(3)
+
+    y_copy().wait_recv()
+    out[:, :HALF] = summed[0] + from_y[...]
+    for q in range(4):
+        for h in range(2):
+            def arrive():
+                ref = from_xyb.at[q * 2 + h]
+                pltpu.make_async_copy(ref, ref, xyb_recv.at[q * 2 + h]).wait()
+
+            pl.when(sender != q * 2 + h)(arrive)
+        out[:, HALF + q * FINE:HALF + q * FINE + FINE] = from_xyb[q * 2] + from_xyb[q * 2 + 1]
 
     many = 32 * KPARTS
 
@@ -315,25 +417,15 @@
         left = landed.at[pl.ds(0, many)]
         pltpu.make_async_copy(left, left, send_sem).wait()
 
-    for t in range(STEPS):
-        for k in range(KPARTS):
-            forward(t, kind, k, pair, pair_send.at[t, k]).wait_send()
-            forward(t, kind, k, sibling, sib_send.at[t, 0, k]).wait_send()
-            forward(t, 1 - kind, k, sibling, sib_send.at[t, 1, k]).wait_send()
-        for n in range(tiles):
-            for d in range(1, 4):
-                z_copy(t, n, d).wait_send()
-            for kk in range(2):
-                d, cp = x_copy(t, n, kk)
-                pl.when(d != 0)(cp.wait_send)
-    for n in range(tiles):
-        y_copy(n).wait_send()
+    end_sends(3)
+    end_sums(2)
+    end_sums(3)
+    y_copy().wait_send()
 
 
 def per_device(amplitudes, integrals):
     ab, cols = integrals.shape
     part = cols // KPARTS
-    tiles = ab // WIDE
     return pl.pallas_call(
         kernel,
         out_shape=jax.ShapeDtypeStruct((PIECE, ab), jnp.float32),
@@ -344,24 +436,37 @@
             pltpu.VMEM((32 * KPARTS, ROWS, part), jnp.bfloat16),
             pltpu.VMEM((BLOCK, min(part, 512)), jnp.float32),
             pltpu.VMEM((MPARTS, STEPS * STEP, cols // MPARTS), jnp.bfloat16),
-            pltpu.VMEM((STEPS, 4, tiles, 2 * PIECE, WIDE), jnp.float32),
-            pltpu.VMEM((STEPS, 3, tiles, 2 * PIECE, WIDE), jnp.float32),
-            pltpu.VMEM((STEPS, tiles, 2 * PIECE, WIDE), jnp.float32),
-            pltpu.VMEM((2, 3, tiles, PIECE, WIDE), jnp.float32),
-            pltpu.VMEM((2, tiles, PIECE, WIDE), jnp.float32),
-            pltpu.VMEM((tiles, PIECE, WIDE), jnp.float32),
+            pltpu.VMEM((STEP, HALF), jnp.float32),
+            pltpu.VMEM((STEPS, 4, 2 * PIECE, HALF), jnp.float32),
+            pltpu.VMEM((STEPS, 3, 2 * PIECE, HALF), jnp.float32),
+            pltpu.VMEM((STEPS, 2 * PIECE, HALF), jnp.float32),
+            pltpu.VMEM((2, 3, PIECE, HALF), jnp.float32),
+            pltpu.VMEM((2, PIECE, HALF), jnp.float32),
+            pltpu.VMEM((PIECE, HALF), jnp.float32),
+            pltpu.VMEM((STEPS, 4, 4, 2 * PIECE, FINE), jnp.float32),
+            pltpu.VMEM((STEPS, 3, 4, 2 * PIECE, FINE), jnp.float32),
+            pltpu.VMEM((STEPS, 4, 2 * PIECE, FINE), jnp.float32),
+            pltpu.VMEM((STEPS, 3, 2 * PIECE, FINE), jnp.float32),
+            pltpu.VMEM((STEPS, 2 * PIECE, FINE), jnp.float32),
+            pltpu.VMEM((8, PIECE, FINE), jnp.float32),
             pltpu.SemaphoreType.DMA,
             pltpu.SemaphoreType.DMA,
             pltpu.SemaphoreType.DMA((STEPS, KPARTS)),
             pltpu.SemaphoreType.DMA((STEPS, KPARTS)),
             pltpu.SemaphoreType.DMA((STEPS, 2, KPARTS)),
             pltpu.SemaphoreType.DMA((STEPS, 4, KPARTS)),
-            pltpu.SemaphoreType.DMA((STEPS, 3, tiles)),
-            pltpu.SemaphoreType.DMA((STEPS, 3, tiles)),
-            pltpu.SemaphoreType.DMA((STEPS, tiles, 2)),
-            pltpu.SemaphoreType.DMA((2, 3, tiles)),
-            pltpu.SemaphoreType.DMA((tiles,)),
-            pltpu.SemaphoreType.DMA((tiles,)),
+            pltpu.SemaphoreType.DMA((STEPS, 3)),
+            pltpu.SemaphoreType.DMA((STEPS, 3)),
+            pltpu.SemaphoreType.DMA((STEPS, 2)),
+            pltpu.SemaphoreType.DMA((2, 3)),
+            pltpu.SemaphoreType.DMA,
+            pltpu.SemaphoreType.DMA,
+            pltpu.SemaphoreType.DMA((STEPS, 3)),
+            pltpu.SemaphoreType.DMA((STEPS, 3)),
+            pltpu.SemaphoreType.DMA((STEPS, 3)),
+            pltpu.SemaphoreType.DMA((STEPS, 3)),
+            pltpu.SemaphoreType.DMA((STEPS, 2)),
+            pltpu.SemaphoreType.DMA((8,)),
         ],
         compiler_params=pltpu.CompilerParams(
             collective_id=0, has_side_effects=True, vmem_limit_bytes=60 * 2**20

time: 117 us -> 110 us (0.940)
  Pallas kernels: 115 us -> 109 us
    pallas_call x1, Pallas kernels: 115 us -> 109 us  [per_device(): pl.pallas_call(kernel, out_shape=jax.ShapeDtypeStruct((PIECE, ab), jnp.fl...]
where the time goes in v3:
time: 110 us
  Pallas kernels  109 us (99%)
  local copies, waits for them, and re-layouts  1.54 us (1%)
    pallas_call x1, Pallas kernels, per_device(): pl.pallas_call(kernel, out_shape=jax.ShapeDtypeStruct((PIECE, ab), jnp.fl...  109 us

profile of v3, /device:TPU:18, one launch (start us, length us, event | category | flops | bytes accessed | tf_op | source)
XLA Modules:
  0.0 110.4 jit_solution(2484324912880540557)
XLA Ops:
  0.0 108.8 %ladder.1 = f32[24,1024]{1,0:T(8,128)} custom-call(bf16[6,262144]{1,0:T(8,128)(2,1)} %amp.1, bf16[1024,8192]{1,0:T(8,128)(2,1)} %integrals_hbm.1), custom_call_target="tpu_custom_call" | custom-call | flops 12884901888 | bytes 16777216 | tf_op jit(solution)/shard_map/ladder/pallas_call | solution.py:429
  108.8 1.5 %copy.4 = f32[24,1024]{1,0:T(8,128)} copy(f32[24,1024]{1,0:T(8,128)} %ladder.1) | data formatting | bytes 196608

commit v4 on v3

v4 whole, which is shorter than its diff:
```python
import jax
import jax.numpy as jnp
from jax import lax
from jax.experimental import pallas as pl
from jax.experimental.pallas import tpu as pltpu
from jax.sharding import PartitionSpec as P

MESH = pl.DeviceIdType.MESH
ROWS = 6
BLOCK = 8 * ROWS
STEP = 4 * BLOCK
STEPS = 4
PIECE = 24
KPARTS = 8
MPARTS = 4
HALF = 512
FINE = 128
AHEAD = 3
GATE = 3
LAG = 2


def device(x, y, z, s):
    return ((y % 2) * 2 + s, (x * 2 + y // 2) * 4 + z)


def across(y):
    return (y + 3 + 2 * (y % 2)) % 4


def kernel(amp, integrals_hbm, out, slabs, integrals, landed, wide, panel, total, parts, from_z, reduced, from_x, summed, from_y,
           parts_b, from_xb, reduced_b, from_zb, summed_b, from_xyb,
           load_sem, send_sem, land_sem, pair_send, sib_send, block_sem, z_send, z_recv, x_send, x_recv, y_send, y_recv,
           xb_send, xb_recv, zb_send, zb_recv, xyb_send, xyb_recv):
    g = lax.axis_index("grp")
    c = lax.axis_index("col")
    x, y, z, s = c // 8, (c // 4) % 2 * 2 + g // 2, c % 4, g % 2
    y_hi, y_lo = y // 2, y % 2
    kind = (y_lo + y_hi) % 2
    cols = integrals.shape[0]
    part = cols // KPARTS
    per = KPARTS // MPARTS
    core = x % 2
    own = jnp.where(s == core, 1, 0)
    pair = device(x, y + 1 - 2 * y_lo, z, s)
    sibling = device(x, y, z, 1 - s)

    bar = pltpu.get_barrier_semaphore()

    across_lo, across_hi = 1 - y_lo, 1 - y_hi

    def hello(grp, col):
        pl.semaphore_signal(bar, inc=1, device_id=(grp, col), device_id_type=MESH)

    start_x = x + 1 - own

    def greet(i, _):
        src_x = lax.rem(start_x + 2 * lax.div(i, 4), 4)
        src_z = lax.rem(z + lax.rem(i, 4), 4)
        for src_s in range(2):
            hello(across_lo * 2 + src_s, src_x * 8 + across_hi * 4 + src_z)
            hello(y_lo * 2 + src_s, src_x * 8 + y_hi * 4 + src_z)
        return 0

    lax.fori_loop(1, 8, greet, 0)
    first_x = lax.rem(start_x, 4)
    for src_s in range(2):
        hello(across_lo * 2 + src_s, first_x * 8 + across_hi * 4 + z)
    hello(y_lo * 2 + 1 - s, first_x * 8 + y_hi * 4 + z)

    @pl.when(own == 0)
    def _():
        hello(y_lo * 2 + s, first_x * 8 + y_hi * 4 + z)

    hello(across_lo * 2 + s, c)
    hello(y_lo * 2 + 1 - s, c)
    for d in range(1, 4):
        hello(g, c - z + lax.rem(z + d, 4))
        hello(g, lax.rem(x + d, 4) * 8 + y_hi * 4 + z)
        hello(g, lax.rem(x + d, 4) * 8 + across_hi * 4 + z)
    hello(g, x * 8 + across_hi * 4 + z)
    slab = slabs.shape[1]
    n_slabs = integrals_hbm.shape[0] // slab

    def slab_copy(i):
        rows = pl.ds(pl.multiple_of(i * slab, slab), slab)
        return pltpu.make_async_copy(integrals_hbm.at[rows], slabs.at[i % 2], load_sem.at[i % 2])

    def turn_slab(i):
        slab_copy(i).wait()
        width = 1024

        def one(n, _):
            lanes = pl.ds(pl.multiple_of(n * width, width), width)
            integrals[lanes, pl.ds(i * slab, slab)] = slabs[i % 2, :, lanes].T
            return 0

        lax.fori_loop(0, cols // width, one, 0)
        if i + 2 < n_slabs:
            slab_copy(i + 2).start()

    parts[...] = jnp.zeros_like(parts)
    parts_b[...] = jnp.zeros_like(parts_b)
    pl.semaphore_wait(bar, 44 - own)

    my_step = s * 2 + x // 2

    mine_slot = my_step * KPARTS * 8 + y_hi * 4 + z
    here_grp, across_grp = y_lo * 2 + core, across_lo * 2 + core

    def send_part(k):
        dst = landed.at[mine_slot + k * 8]
        sem = land_sem.at[my_step, k]

        def columns(col):
            return amp.at[:, pl.ds(pl.multiple_of(col * cols + k * part, 128), part)]

        def send(grp, col):
            pltpu.make_async_remote_copy(
                src_ref=columns(col), dst_ref=dst, send_sem=send_sem, recv_sem=sem,
                device_id=(grp, col), device_id_type=MESH,
            ).start()

        @pl.when(own == 1)
        def _():
            pltpu.make_async_copy(columns(c), dst, sem).start()

        @pl.when(own == 0)
        def _():
            send(here_grp, c)

        send(across_grp, x * 8 + across_hi * 4 + z)

        def one(j, _):
            dx = lax.rem(j, 4)
            dz = lax.div(j, 4) + dx
            send(here_grp, lax.rem(x + dx, 4) * 8 + y_hi * 4 + lax.rem(z + dz, 4))
            send(across_grp, lax.rem(x - dx + 4, 4) * 8 + across_hi * 4 + lax.rem(z - dz + 8, 4))
            return 0

        lax.fori_loop(1, 16, one, 0)

    def send_parts(who, first, last):
        if first < last:
            @pl.when(s == who)
            def _():
                lax.fori_loop(first, last, lambda k, _: (send_part(k), 0)[1], 0)

    def block_ref(t, kk, ss, k):
        rows = pl.ds(pl.multiple_of(t * STEP + kk * 2 * BLOCK + ss * BLOCK, 16), BLOCK)
        return panel.at[k // per, rows, pl.ds(pl.multiple_of(k % per * part, 128), part)]

    def forward(t, kk, k, to, sem):
        ref = block_ref(t, kk, s, k)
        return pltpu.make_async_remote_copy(
            src_ref=ref, dst_ref=ref, send_sem=sem, recv_sem=block_sem.at[t, kk * 2 + s, k],
            device_id=to, device_id_type=MESH,
        )

    def wait_block(t, kk, ss, k):
        ref = block_ref(t, kk, ss, k)
        pltpu.make_async_copy(ref, ref, block_sem.at[t, kk * 2 + ss, k]).wait()

    def take(t, k):
        base = (t * KPARTS + k) * 8
        eight = landed.at[pl.ds(base, 8)]
        pltpu.make_async_copy(eight, eight, land_sem.at[t, k]).wait()
        row0 = pl.multiple_of(t * STEP + kind * 2 * BLOCK + s * BLOCK, 16)
        width = min(part, 512)

        def repack(i, _):
            lanes = pl.ds(pl.multiple_of(i * width, width), width)
            to = pl.ds(pl.multiple_of(k % per * part + i * width, width), width)
            for m in range(8):
                wide[pl.ds(m * ROWS, ROWS), :] = landed[base + m, :, lanes].astype(jnp.float32)
            panel[k // per, pl.ds(row0, BLOCK), to] = wide[...].astype(jnp.bfloat16)
            return 0

        lax.fori_loop(0, part // width, repack, 0)
        forward(t, kind, k, pair, pair_send.at[t, k]).start()
        forward(t, kind, k, sibling, sib_send.at[t, 0, k]).start()

    def relay(t, k):
        wait_block(t, 1 - kind, s, k)
        forward(t, 1 - kind, k, sibling, sib_send.at[t, 1, k]).start()

    def wait_sibling(t, k):
        wait_block(t, kind, 1 - s, k)
        wait_block(t, 1 - kind, 1 - s, k)

    def z_copy(t, kk, d):
        return pltpu.make_async_remote_copy(
            src_ref=parts.at[t, kk, lax.rem(z + d, 4)], dst_ref=from_z.at[t, kk, d - 1],
            send_sem=z_send.at[t, kk, d - 1], recv_sem=z_recv.at[t, kk, d - 1],
            device_id=(g, c - z + lax.rem(z + d, 4)), device_id_type=MESH,
        )

    def xb_copy(t, kk, d):
        return pltpu.make_async_remote_copy(
            src_ref=parts_b.at[t, kk, lax.rem(x + d, 4)], dst_ref=from_xb.at[t, kk, d - 1],
            send_sem=xb_send.at[t, kk, d - 1], recv_sem=xb_recv.at[t, kk, d - 1],
            device_id=(g, lax.rem(x + d, 4) * 8 + y_hi * 4 + z), device_id_type=MESH,
        )

    def multiply(t, km, kk=None):
        width = per * part
        last = km == MPARTS - 1
        rows = STEP if kk is None else STEP // 2
        row0 = t * STEP + (0 if kk is None else kk * (2 * BLOCK))
        kinds = (0, 1) if kk is None else (kk,)

        def half(n, _):
            total[0:rows, :] = lax.dot_general(
                panel[km, pl.ds(pl.multiple_of(row0, 16), rows), :],
                integrals[pl.ds(pl.multiple_of(km * width, width), width), pl.ds(pl.multiple_of(n * HALF, HALF), HALF)],
                (((1,), (0,)), ((), ())),
                preferred_element_type=jnp.float32,
            )

            @pl.when(n == 0)
            def _():
                for i, kind_i in enumerate(kinds):
                    for r in range(2):
                        for u in range(2):
                            row = (i * 2 + r) * BLOCK + u * PIECE
                            parts[t, kind_i, 2 * r + u] += total[row:row + PIECE, :]

                @pl.when(last)
                def _():
                    for kind_i in kinds:
                        for d in (2, 1, 3):
                            z_copy(t, kind_i, d).start()

            @pl.when(n == 1)
            def _():
                for i, kind_i in enumerate(kinds):
                    for q in range(4):
                        for r in range(2):
                            for u in range(2):
                                row = (i * 2 + r) * BLOCK + u * PIECE
                                parts_b[t, kind_i, q, 2 * r + u] += total[row:row + PIECE, q * FINE:q * FINE + FINE]

                @pl.when(last)
                def _():
                    for kind_i in kinds:
                        for d in (2, 1, 3):
                            xb_copy(t, kind_i, d).start()

            return 0

        lax.fori_loop(0, 2, half, 0)

    def multiply_steps(first, last, km):
        lax.fori_loop(first, last, lambda t, _: (multiply(t, km), 0)[1], 0)

    u = z % 2

    def owner_x(t, kk):
        return 2 * ((kk + u) % 2) + t // 2

    def x_copy(t, kk):
        d = (owner_x(t, kk) - x + 4) % 4
        place = jnp.maximum(d, 1) - 1
        return d, pltpu.make_async_remote_copy(
            src_ref=reduced.at[t, kk], dst_ref=from_x.at[t % 2, place],
            send_sem=x_send.at[t, kk], recv_sem=x_recv.at[t % 2, place],
            device_id=device(owner_x(t, kk), y, z, s), device_id_type=MESH,
        )

    def y_copy():
        return pltpu.make_async_remote_copy(
            src_ref=summed.at[1], dst_ref=from_y, send_sem=y_send, recv_sem=y_recv,
            device_id=device(x, (y + 2) % 4, z, s), device_id_type=MESH,
        )

    def reduce_z(t, kk):
        for d in range(1, 4):
            z_copy(t, kk, d).wait_recv()
        reduced[t, kk] = 0.5 * (parts[t, kk, z] + from_z[t, kk, 0] + from_z[t, kk, 1] + from_z[t, kk, 2])
        d, cp = x_copy(t, kk)
        pl.when(d != 0)(cp.start)

    def reduce_x(t):
        @pl.when(x % 2 == t // 2)
        def _():
            kk = (x // 2 + u) % 2
            mine = jnp.where(y_hi == t % 2, 0, 1)
            for d in range(3):
                ref = from_x.at[t % 2, d]
                pltpu.make_async_copy(ref, ref, x_recv.at[t % 2, d]).wait()
            summed[mine] = reduced[t, kk] + from_x[t % 2, 0] + from_x[t % 2, 1] + from_x[t % 2, 2]
            pl.when(mine == 1)(y_copy().start)

    def zb_copy(t, kk, d):
        return pltpu.make_async_remote_copy(
            src_ref=reduced_b.at[t, kk, lax.rem(z + d, 4)], dst_ref=from_zb.at[t, kk, d - 1],
            send_sem=zb_send.at[t, kk, d - 1], recv_sem=zb_recv.at[t, kk, d - 1],
            device_id=(g, c - z + lax.rem(z + d, 4)), device_id_type=MESH,
        )

    def reduce_xb(t, kk):
        for d in range(1, 4):
            xb_copy(t, kk, d).wait_recv()
        reduced_b[t, kk] = 0.5 * (
            parts_b[t, kk, x] + from_xb[t, kk, 0] + from_xb[t, kk, 1] + from_xb[t, kk, 2])
        for d in (2, 1, 3):
            zb_copy(t, kk, d).start()

    sender = x * 2 + y_hi

    def xyb_copy(t, kk):
        to_x = owner_x(t, kk)
        here = (to_x == x) & (y_hi == t % 2)
        return here, pltpu.make_async_remote_copy(
            src_ref=summed_b.at[t, kk], dst_ref=from_xyb.at[sender],
            send_sem=xyb_send.at[t, kk], recv_sem=xyb_recv.at[sender],
            device_id=device(to_x, (t % 2) * 2 + y_lo, z, s), device_id_type=MESH,
        )

    def reduce_zb(t, kk):
        for d in range(1, 4):
            zb_copy(t, kk, d).wait_recv()
        summed_b[t, kk] = reduced_b[t, kk, z] + from_zb[t, kk, 0] + from_zb[t, kk, 1] + from_zb[t, kk, 2]
        here, cp = xyb_copy(t, kk)
        pl.when(jnp.logical_not(here))(cp.start)

        @pl.when(here)
        def _():
            from_xyb[sender] = summed_b[t, kk]

    def both_kinds(what, t):
        lax.fori_loop(0, 2, lambda kk, _: (what(t, kk), 0)[1], 0)

    def end_sends(t):
        def one(k, _):
            forward(t, kind, k, pair, pair_send.at[t, k]).wait_send()
            forward(t, kind, k, sibling, sib_send.at[t, 0, k]).wait_send()
            forward(t, 1 - kind, k, sibling, sib_send.at[t, 1, k]).wait_send()
            return 0

        lax.fori_loop(0, KPARTS, one, 0)

    def end_sums_of(t, kk):
        for d in range(1, 4):
            z_copy(t, kk, d).wait_send()
            xb_copy(t, kk, d).wait_send()
            zb_copy(t, kk, d).wait_send()
        d, cp = x_copy(t, kk)
        pl.when(d != 0)(cp.wait_send)
        here, cp = xyb_copy(t, kk)
        pl.when(jnp.logical_not(here))(cp.wait_send)

    def end_sums(t):
        both_kinds(end_sums_of, t)

    def both_first(km):
        for kt in range(km * per, km * per + per):
            wait_sibling(0, kt)
            wait_sibling(1, kt)
        multiply_steps(0, 2, km)

    send_parts(0, 0, AHEAD)
    for k in range(KPARTS):
        take(0, k)
        take(1, k)
        send_parts(0, k + AHEAD, min(k + AHEAD + 1, KPARTS))
        if k >= GATE:
            send_parts(1, k - GATE, k - GATE + 1)
        if k >= LAG:
            relay(0, k - LAG)
            relay(1, k - LAG)
        if k == 0:
            slab_copy(0).start()
            slab_copy(1).start()
        if 1 <= k <= n_slabs // 2:
            turn_slab(2 * k - 2)
            turn_slab(2 * k - 1)
        done = k - LAG - 1
        if done >= 0 and done % per == per - 1:
            both_first(done // per)
    send_parts(1, KPARTS - GATE, KPARTS)
    begun = (KPARTS - LAG - 1) // per
    for k in range(KPARTS):
        take(2, k)
        if k < LAG:
            relay(0, KPARTS - LAG + k)
            relay(1, KPARTS - LAG + k)
        if k >= LAG and (k - LAG) % 2 == 0 and begun + (k - LAG) // 2 < MPARTS:
            both_first(begun + (k - LAG) // 2)

    def third(km, _):
        def one(i, _):
            take(3, km * per + i)
            relay(2, km * per + i)
            return 0

        lax.fori_loop(0, per, one, 0)
        lax.fori_loop(0, per, lambda i, _: (wait_sibling(2, km * per + i), 0)[1], 0)
        multiply(2, km)

        @pl.when(km < 2)
        def _():
            both_kinds(reduce_z, km)
            both_kinds(reduce_xb, km)

        @pl.when(km >= 2)
        def _():
            reduce_x(km - 2)
            both_kinds(reduce_zb, km - 2)

        return 0

    lax.fori_loop(0, MPARTS, third, 0)

    def fourth(km, _):
        @pl.when(km < 2)
        def _():
            def own_kind(i, _):
                m = km * 2 + i
                lax.fori_loop(0, per, lambda i, _: (wait_block(3, kind, 1 - s, m * per + i), 0)[1], 0)
                multiply(3, m, kind)
                return 0

            lax.fori_loop(0, MPARTS // 2, own_kind, 0)

        @pl.when(km == 2)
        def _():
            both_kinds(reduce_z, 2)
            both_kinds(reduce_xb, 2)
            end_sends(0)
            end_sends(1)

        @pl.when(km == 3)
        def _():
            reduce_z(3, kind)
            reduce_xb(3, kind)
            reduce_x(2)
            both_kinds(reduce_zb, 2)
            end_sums(0)
            end_sums(1)

        lax.fori_loop(0, per, lambda i, _: (relay(3, km * per + i), 0)[1], 0)
        lax.fori_loop(0, per, lambda i, _: (wait_block(3, 1 - kind, 1 - s, km * per + i), 0)[1], 0)
        multiply(3, km, 1 - kind)
        return 0

    lax.fori_loop(0, MPARTS, fourth, 0)
    reduce_zb(3, kind)
    reduce_z(3, 1 - kind)
    reduce_xb(3, 1 - kind)
    reduce_x(3)
    reduce_zb(3, 1 - kind)

    y_copy().wait_recv()
    out[:, :HALF] = summed[0] + from_y[...]
    for q in range(4):
        for h in range(2):
            def arrive():
                ref = from_xyb.at[q * 2 + h]
                pltpu.make_async_copy(ref, ref, xyb_recv.at[q * 2 + h]).wait()

            pl.when(sender != q * 2 + h)(arrive)
        out[:, HALF + q * FINE:HALF + q * FINE + FINE] = from_xyb[q * 2] + from_xyb[q * 2 + 1]

    many = 32 * KPARTS

    @pl.when(own == 1)
    def _():
        left = landed.at[pl.ds(0, many - KPARTS)]
        pltpu.make_async_copy(left, left, send_sem).wait()

    @pl.when(own == 0)
    def _():
        left = landed.at[pl.ds(0, many)]
        pltpu.make_async_copy(left, left, send_sem).wait()

    end_sends(2)
    end_sends(3)
    end_sums(2)
    end_sums(3)
    y_copy().wait_send()


def per_device(amplitudes, integrals):
    ab, cols = integrals.shape
    part = cols // KPARTS
    return pl.pallas_call(
        kernel,
        out_shape=jax.ShapeDtypeStruct((PIECE, ab), jnp.float32),
        in_specs=[pl.BlockSpec(memory_space=pl.ANY)] * 2,
        out_specs=pl.BlockSpec(memory_space=pltpu.VMEM),
        scratch_shapes=[
            pltpu.VMEM((2, ab // 8, cols), jnp.bfloat16),
            pltpu.VMEM((cols, ab), jnp.bfloat16),
            pltpu.VMEM((32 * KPARTS, ROWS, part), jnp.bfloat16),
            pltpu.VMEM((BLOCK, min(part, 512)), jnp.float32),
            pltpu.VMEM((MPARTS, STEPS * STEP, cols // MPARTS), jnp.bfloat16),
            pltpu.VMEM((STEP, HALF), jnp.float32),
            pltpu.VMEM((STEPS, 2, 4, PIECE, HALF), jnp.float32),
            pltpu.VMEM((STEPS, 2, 3, PIECE, HALF), jnp.float32),
            pltpu.VMEM((STEPS, 2, PIECE, HALF), jnp.float32),
            pltpu.VMEM((2, 3, PIECE, HALF), jnp.float32),
            pltpu.VMEM((2, PIECE, HALF), jnp.float32),
            pltpu.VMEM((PIECE, HALF), jnp.float32),
            pltpu.VMEM((STEPS, 2, 4, 4, PIECE, FINE), jnp.float32),
            pltpu.VMEM((STEPS, 2, 3, 4, PIECE, FINE), jnp.float32),
            pltpu.VMEM((STEPS, 2, 4, PIECE, FINE), jnp.float32),
            pltpu.VMEM((STEPS, 2, 3, PIECE, FINE), jnp.float32),
            pltpu.VMEM((STEPS, 2, PIECE, FINE), jnp.float32),
            pltpu.VMEM((8, PIECE, FINE), jnp.float32),
            pltpu.SemaphoreType.DMA((2,)),
            pltpu.SemaphoreType.DMA,
            pltpu.SemaphoreType.DMA((STEPS, KPARTS)),
            pltpu.SemaphoreType.DMA((STEPS, KPARTS)),
            pltpu.SemaphoreType.DMA((STEPS, 2, KPARTS)),
            pltpu.SemaphoreType.DMA((STEPS, 4, KPARTS)),
            pltpu.SemaphoreType.DMA((STEPS, 2, 3)),
            pltpu.SemaphoreType.DMA((STEPS, 2, 3)),
            pltpu.SemaphoreType.DMA((STEPS, 2)),
            pltpu.SemaphoreType.DMA((2, 3)),
            pltpu.SemaphoreType.DMA,
            pltpu.SemaphoreType.DMA,
            pltpu.SemaphoreType.DMA((STEPS, 2, 3)),
            pltpu.SemaphoreType.DMA((STEPS, 2, 3)),
            pltpu.SemaphoreType.DMA((STEPS, 2, 3)),
            pltpu.SemaphoreType.DMA((STEPS, 2, 3)),
            pltpu.SemaphoreType.DMA((STEPS, 2)),
            pltpu.SemaphoreType.DMA((8,)),
        ],
        compiler_params=pltpu.CompilerParams(
            collective_id=0, has_side_effects=True, vmem_limit_bytes=60 * 2**20
        ),
        cost_estimate=pl.CostEstimate(
            flops=2 * STEPS * STEP * ab * cols, bytes_accessed=2 * ab * cols, transcendentals=0
        ),
        name="ladder",
    )(amplitudes, integrals)


def solution(mesh):
    return jax.shard_map(
        per_device,
        mesh=mesh,
        in_specs=(P(("grp", "col"), None), P("grp", "col")),
        out_specs=P("col", "grp"),
        check_vma=False,
    )
```

time: 110 us -> 107 us (0.973); the launches traced: 110 us -> 105 us
  Pallas kernels: 109 us -> 104 us
    pallas_call x1, Pallas kernels: 109 us -> 104 us  [per_device(): pl.pallas_call(kernel, out_shape=jax.ShapeDtypeStruct((PIECE, ab), jnp.fl...]
where the time goes in v4:
time: 107 us; the launch traced here: 105 us
  Pallas kernels  104 us (97%)
  local copies, waits for them, and re-layouts  1.54 us (1%)
    pallas_call x1, Pallas kernels, per_device(): pl.pallas_call(kernel, out_shape=jax.ShapeDtypeStruct((PIECE, ab), jnp.fl...  104 us

profile of v4, /device:TPU:18, one launch (start us, length us, event | category | flops | bytes accessed | tf_op | source)
XLA Modules:
  0.0 105.1 jit_solution(6211882188926229480)
XLA Ops:
  0.0 103.6 %ladder.1 = f32[24,1024]{1,0:T(8,128)} custom-call(bf16[6,262144]{1,0:T(8,128)(2,1)} %amp.1, bf16[1024,8192]{1,0:T(8,128)(2,1)} %integrals_hbm.1), custom_call_target="tpu_custom_call" | custom-call | flops 12884901888 | bytes 16777216 | tf_op jit(solution)/shard_map/ladder/pallas_call | solution.py:487
  103.6 1.5 %copy.4 = f32[24,1024]{1,0:T(8,128)} copy(f32[24,1024]{1,0:T(8,128)} %ladder.1) | data formatting | bytes 196608

commit v5 on v4

--- a/solution.py
+++ b/solution.py
@@ -15,7 +15,7 @@
 MPARTS = 4
 HALF = 512
 FINE = 128
-AHEAD = 3
+AHEAD = 5
 GATE = 3
 LAG = 2
 
@@ -352,6 +352,19 @@
 
     def end_sums(t):
         both_kinds(end_sums_of, t)
+
+    def end_direct():
+        many = 32 * KPARTS
+
+        @pl.when(own == 1)
+        def _():
+            left = landed.at[pl.ds(0, many - KPARTS)]
+            pltpu.make_async_copy(left, left, send_sem).wait()
+
+        @pl.when(own == 0)
+        def _():
+            left = landed.at[pl.ds(0, many)]
+            pltpu.make_async_copy(left, left, send_sem).wait()
 
     def both_first(km):
         for kt in range(km * per, km * per + per):
@@ -413,6 +426,11 @@
     lax.fori_loop(0, MPARTS, third, 0)
 
     def fourth(km, _):
+        def relays(first, last):
+            lax.fori_loop(first, last, lambda i, _: (relay(3, km * per + i), 0)[1], 0)
+
+        relays(0, 1)
+
         @pl.when(km < 2)
         def _():
             def own_kind(i, _):
@@ -436,20 +454,24 @@
             reduce_xb(3, kind)
             reduce_x(2)
             both_kinds(reduce_zb, 2)
-            end_sums(0)
-            end_sums(1)
-
-        lax.fori_loop(0, per, lambda i, _: (relay(3, km * per + i), 0)[1], 0)
+
+        relays(1, per)
         lax.fori_loop(0, per, lambda i, _: (wait_block(3, 1 - kind, 1 - s, km * per + i), 0)[1], 0)
         multiply(3, km, 1 - kind)
         return 0
 
     lax.fori_loop(0, MPARTS, fourth, 0)
     reduce_zb(3, kind)
+    end_sums(0)
+    end_sends(2)
     reduce_z(3, 1 - kind)
     reduce_xb(3, 1 - kind)
+    end_sums(1)
     reduce_x(3)
     reduce_zb(3, 1 - kind)
+    end_sends(3)
+    end_sums(2)
+    end_direct()
 
     y_copy().wait_recv()
     out[:, :HALF] = summed[0] + from_y[...]
@@ -462,22 +484,7 @@
             pl.when(sender != q * 2 + h)(arrive)
         out[:, HALF + q * FINE:HALF + q * FINE + FINE] = from_xyb[q * 2] + from_xyb[q * 2 + 1]
 
-    many = 32 * KPARTS
-
-    @pl.when(own == 1)
-    def _():
-        left = landed.at[pl.ds(0, many - KPARTS)]
-        pltpu.make_async_copy(left, left, send_sem).wait()
-
-    @pl.when(own == 0)
-    def _():
-        left = landed.at[pl.ds(0, many)]
-        pltpu.make_async_copy(left, left, send_sem).wait()
-
-    end_sends(2)
-    end_sends(3)
-    end_sums(2)
-    end_sums(3)
+    both_kinds(end_sums_of, 3)
     y_copy().wait_send()
 
 

time: 107 us -> 105 us (0.981); the launches traced: 105 us -> 105 us
  no operation moved by 1% of the time
where the time goes in v5:
time: 105 us
  Pallas kernels  103 us (98%)
  local copies, waits for them, and re-layouts  1.54 us (1%)
    pallas_call x1, Pallas kernels, per_device(): pl.pallas_call(kernel, out_shape=jax.ShapeDtypeStruct((PIECE, ab), jnp.fl...  103 us

profile of v5, /device:TPU:18, one launch (start us, length us, event | category | flops | bytes accessed | tf_op | source)
XLA Modules:
  0.0 104.5 jit_solution(18221333232345528181)
XLA Ops:
  0.0 103.0 %ladder.1 = f32[24,1024]{1,0:T(8,128)} custom-call(bf16[6,262144]{1,0:T(8,128)(2,1)} %amp.1, bf16[1024,8192]{1,0:T(8,128)(2,1)} %integrals_hbm.1), custom_call_target="tpu_custom_call" | custom-call | flops 12884901888 | bytes 16777216 | tf_op jit(solution)/shard_map/ladder/pallas_call | solution.py:494
  103.0 1.5 %copy.4 = f32[24,1024]{1,0:T(8,128)} copy(f32[24,1024]{1,0:T(8,128)} %ladder.1) | data formatting | bytes 196608

commit v6 on v5

--- a/solution.py
+++ b/solution.py
@@ -402,12 +402,11 @@
             both_first(begun + (k - LAG) // 2)
 
     def third(km, _):
-        def one(i, _):
-            take(3, km * per + i)
-            relay(2, km * per + i)
-            return 0
-
-        lax.fori_loop(0, per, one, 0)
+        @pl.when(km < MPARTS // 2)
+        def _():
+            lax.fori_loop(0, 2 * per, lambda i, _: (take(3, km * 2 * per + i), 0)[1], 0)
+
+        lax.fori_loop(0, per, lambda i, _: (relay(2, km * per + i), 0)[1], 0)
         lax.fori_loop(0, per, lambda i, _: (wait_sibling(2, km * per + i), 0)[1], 0)
         multiply(2, km)
 

time: 105 us -> 105 us (level)
  no operation moved by 1% of the time
where the time goes in v6:
time: 105 us; the launch traced here: 104 us
  Pallas kernels  103 us (98%)
  local copies, waits for them, and re-layouts  1.54 us (1%)
    pallas_call x1, Pallas kernels, per_device(): pl.pallas_call(kernel, out_shape=jax.ShapeDtypeStruct((PIECE, ab), jnp.fl...  103 us

profile of v6, /device:TPU:18, one launch (start us, length us, event | category | flops | bytes accessed | tf_op | source)
XLA Modules:
  0.0 104.1 jit_solution(10451459500924435127)
XLA Ops:
  0.0 102.6 %ladder.1 = f32[24,1024]{1,0:T(8,128)} custom-call(bf16[6,262144]{1,0:T(8,128)(2,1)} %amp.1, bf16[1024,8192]{1,0:T(8,128)(2,1)} %integrals_hbm.1), custom_call_target="tpu_custom_call" | custom-call | flops 12884901888 | bytes 16777216 | tf_op jit(solution)/shard_map/ladder/pallas_call | solution.py:493
  102.6 1.5 %copy.4 = f32[24,1024]{1,0:T(8,128)} copy(f32[24,1024]{1,0:T(8,128)} %ladder.1) | data formatting | bytes 196608
